TPU v7x, 32 devices: a whole 2x2x4 slice. The times are simulated.
32 devices in a mesh: leaf: 8 (over y, x, core), front: 4 (over z).
Axes of the slice: x: 2, y: 2, z: 4, core: 2. Of those that a mesh axis runs over, the one named last changes fastest.
Arguments:
- child_left_factors: bfloat16 [8, 6144, 128], P('leaf', 'front'), may hold values from -0.078125 to 0.078125
- child_v: bfloat16 [8, 6144, 128], P('leaf', 'front'), may hold values from -0.1875 to 0.1875
- ranks: int32 [8, 12], P('leaf', 'front'), may hold values from 8 to 128
- sketch: bfloat16 [6144, 128], P('front'), may hold values from -0.078125 to 0.078125
- dinv: bfloat16 [8, 12, 512, 512], P('leaf', 'front'), may hold values from -1 to 3, as said below
- rhs: bfloat16 [8, 64, 6144], P('leaf', None, 'front'), may hold values from -6 to 6
Outputs:
- solution: float32 [8, 64, 6144], P('leaf', None, 'front')
Inputs may be any that keep to these rules, and one draw needn't show every extreme that they name: `ranks`: rank of each 512-row tile of a contribution block; columns of child_left_factors at or beyond it do not count. `dinv`: each [512, 512] block is the inverse of a diagonal tile of a factored front.
All inputs are finite; a program needn't handle non-finite values.
Results may differ from a plain program's by a relative error of at most 0.0045.
Values may be sent and summed in bfloat16 or wider, within the bound.
A program may use at most 64 MiB of HBM per device.

v0:
```python
import jax
import jax.numpy as jnp
from jax import lax
from jax.sharding import PartitionSpec as P


def partner(value, axis, distance):
    return lax.ppermute(value, axis, [(i, i ^ 1 << distance) for i in range(lax.axis_size(axis))])


def passed_along(value, axis, steps):
    count = lax.axis_size(axis)
    first, last = (max(0, -steps), min(count, count - steps))
    return lax.ppermute(value, axis, [(source, source + steps) for source in range(first, last)])


def masked_rows(child_left_factors, ranks):
    tile = child_left_factors.shape[1] // ranks.shape[1]
    rank_of_rows = jnp.repeat(ranks, tile, axis=1)
    keep = lax.broadcasted_iota(jnp.int32, child_left_factors.shape, 2) < rank_of_rows[:, :, None]
    return jnp.where(keep, child_left_factors, jnp.zeros_like(child_left_factors))


def right_solve(factor, matrix):
    return jax.vmap(
        lambda factor_one, block_one: jax.scipy.linalg.solve_triangular(
            factor_one, block_one.T, lower=True
        ).T
    )(factor, matrix)


def merge_pairs(first_u, first_v, second_u, second_v, sketch):
    highest = lax.Precision.HIGHEST
    proj_first = jnp.einsum("kmr,ms->krs", first_v, sketch, preferred_element_type=jnp.float32)
    proj_second = jnp.einsum("kmr,ms->krs", second_v, sketch, preferred_element_type=jnp.float32)
    proj_first, proj_second = lax.psum((proj_first, proj_second), "front")
    sample = jnp.einsum(
        "kmr,krs->kms", first_u, proj_first.astype(jnp.bfloat16), preferred_element_type=jnp.float32
    )
    sample = sample + jnp.einsum(
        "kmr,krs->kms",
        second_u,
        proj_second.astype(jnp.bfloat16),
        preferred_element_type=jnp.float32,
    )
    gram_local = jnp.einsum("kms,kmt->kst", sample, sample, precision=highest)
    gram = lax.psum(gram_local, "front")
    factor = jnp.linalg.cholesky(gram)
    basis = right_solve(factor, sample)
    weight_first = jnp.einsum(
        "kmr,kms->krs", first_u, basis, precision=highest, preferred_element_type=jnp.float32
    )
    second_weight = jnp.einsum(
        "kmr,kms->krs", second_u, basis, precision=highest, preferred_element_type=jnp.float32
    )
    weight_first, second_weight = lax.psum((weight_first, second_weight), "front")
    new_v = jnp.einsum(
        "kmr,krs->kms",
        first_v,
        weight_first.astype(jnp.bfloat16),
        preferred_element_type=jnp.float32,
    )
    new_v = new_v + jnp.einsum(
        "kmr,krs->kms",
        second_v,
        second_weight.astype(jnp.bfloat16),
        preferred_element_type=jnp.float32,
    )
    return (basis.astype(jnp.bfloat16), new_v.astype(jnp.bfloat16))


def on_device(child_left_factors, child_v, ranks, sketch, dinv, rhs):
    own_u = masked_rows(child_left_factors, ranks)
    sibling_u, sibling_v = partner((own_u, child_v), "leaf", 0)
    pair_u, pair_v = merge_pairs(own_u, child_v, sibling_u, sibling_v, sketch)
    cousin_u, cousin_v = partner((pair_u, pair_v), "leaf", 1)
    group_u, group_v = merge_pairs(pair_u, pair_v, cousin_u, cousin_v, sketch)
    tile_inv = dinv[0]
    tile_count = tile_inv.shape[0]
    tile_rows = tile_inv.shape[1]
    left_f = group_u[0]
    right_f = group_v[0]
    sides = rhs[0]
    sides_count = sides.shape[0]
    rank_width = left_f.shape[1]
    coupled_blocks = jnp.einsum(
        "tij,tjr->tir",
        tile_inv,
        left_f.reshape(tile_count, tile_rows, rank_width),
        preferred_element_type=jnp.float32,
    )
    coupled_blocks = coupled_blocks.reshape(tile_count * tile_rows, rank_width).astype(jnp.bfloat16)
    solved_rows = jnp.einsum(
        "htj,tij->hti",
        sides.reshape(sides_count, tile_count, tile_rows),
        tile_inv,
        preferred_element_type=jnp.float32,
    )
    solved_rows = solved_rows.reshape(sides_count, tile_count * tile_rows)
    solved_b = solved_rows.astype(jnp.bfloat16)
    matrix_local = jnp.einsum(
        "mr,ms->rs", right_f, coupled_blocks, preferred_element_type=jnp.float32
    )
    vector_local = jnp.dot(solved_b, right_f, preferred_element_type=jnp.float32)
    matrix, vector = lax.psum((matrix_local, vector_local), "front")
    highest = lax.Precision.HIGHEST

    def advance(current_index, carry):
        current, incoming = carry
        incoming = passed_along(current, "leaf", 1)
        current = vector - jnp.dot(incoming, matrix.T, precision=highest)
        return (current, incoming)

    start = jnp.zeros_like(vector)
    _, previous = lax.fori_loop(0, lax.axis_size("leaf"), advance, (start, start))
    correction = jnp.einsum(
        "hr,mr->hm", previous, coupled_blocks.astype(jnp.float32), precision=highest
    )
    solution = solved_rows - correction
    return solution[None]


def solution(mesh):
    placed = (
        P("leaf", "front", None),
        P("leaf", "front", None),
        P("leaf", "front"),
        P("front", None),
        P("leaf", "front", None, None),
        P("leaf", None, "front"),
    )
    return jax.shard_map(
        on_device, mesh=mesh, in_specs=placed, out_specs=P("leaf", None, "front"), check_vma=False
    )
```

profile of v0, /device:TPU:4, one launch (start us, length us, event | category | flops | bytes accessed | tf_op | source)
XLA Modules:
  0.0 346.2 jit_solution(1477546245287997565)
XLA Ops:
  7.5 1.3 fusion.17
  9.2 1.4 convolution_bitcast_fusion.9
  11.8 21.9 %all-reduce.17 = (bf16[1,128,128]{2,1,0:T(8,128)(2,1)S(1)}, bf16[1,128,128]{2,1,0:T(8,128)(2,1)}) all-reduce(f32[1,128,128]{2,1,0:T(8,128)S(1)} %convolution_bitcast_fusion.9, f32[1,128,128]{2,1,0:T(8,128)S(1)} %convolution_bitcast_fusion.8), channel_id=1, replica_groups=mesh['leaf'=8,'front'=4] {'front'}, use_global_device_ids=true, to_apply=%region_0.1 | all-reduce | flops 32768 | bytes 196608 | tf_op jit(solution)/shard_map/psum | solution.py:36
  34.7 1.3 convolution_add_fusion.3
  36.0 2.0 convolution_bitcast_fusion.1
  38.1 1.3 fusion.5
  39.5 31.0 %all-reduce.12.cloned.1.call-done = f32[1,128,128]{1,2,0:T(8,128)} async-done(((f32[1,128,128]{1,2,0:T(8,128)}), f32[1,128,128]{1,2,0:T(8,128)}) %all-reduce.12.cloned.1.call-update) | async-done | bytes 65552 | tf_op jit(solution)/shard_map/psum | solution.py:47
  72.3 11.7 %custom-call.9 = f32[1,128,128]{2,1,0:T(8,128)S(1)} custom-call(f32[1,128,128]{2,1,0:T(8,128)S(1)} %fusion.43), custom_call_target="Cholesky" | custom-call | tf_op jit(solution)/shard_map/jit(cholesky)/cholesky | solution.py:48
  85.2 10.4 %custom-call.10 = f32[1,1,128,128]{2,3,1,0:T(8,128)} custom-call(f32[1,1,128,128]{3,2,1,0:T(8,128)S(1)} %fusion.38), custom_call_target="InvertDiagBlocksLowerTriangular" | custom-call | tf_op jit(solution)/shard_map/vmap(jit(_solve_triangular))/triangular_solve | solution.py:26
  95.7 1.7 fusion.15
  97.4 2.3 convolution_bitcast_fusion.7
  99.7 2.3 convolution_bitcast_fusion.6
  101.9 20.9 %all-reduce.18 = (bf16[1,128,128]{2,1,0:T(8,128)(2,1)}, bf16[1,128,128]{2,1,0:T(8,128)(2,1)}) all-reduce(f32[1,128,128]{2,1,0:T(8,128)} %convolution_bitcast_fusion.7, f32[1,128,128]{2,1,0:T(8,128)} %convolution_bitcast_fusion.6), channel_id=1, replica_groups=mesh['leaf'=8,'front'=4] {'front'}, use_global_device_ids=true, to_apply=%region_5.8 | all-reduce | flops 32768 | bytes 196608 | tf_op jit(solution)/shard_map/psum | solution.py:56
  125.8 1.5 collective-permute-start.4
  128.0 7.9 %collective-permute-done.4 = bf16[1,1536,128]{1,2,0:T(8,128)(2,1)S(1)} collective-permute-done((bf16[1,1536,128]{1,2,0:T(8,128)(2,1)S(1)}, bf16[1,1536,128]{1,2,0:T(8,128)(2,1)S(1)}, u32[]{:S(2)}, u32[]{:S(2)}) %collective-permute-start.4) | collective-permute-done | bytes 393248 | tf_op jit(solution)/shard_map/ppermute | solution.py:8
  137.6 19.2 %all-reduce.19 = (bf16[1,128,128]{2,1,0:T(8,128)(2,1)S(1)}, bf16[1,128,128]{2,1,0:T(8,128)(2,1)}) all-reduce(f32[1,128,128]{2,1,0:T(8,128)} %convolution_bitcast_fusion.5, f32[1,128,128]{2,1,0:T(8,128)} %convolution_bitcast_fusion.4), channel_id=1, replica_groups=mesh['leaf'=8,'front'=4] {'front'}, use_global_device_ids=true, to_apply=%region_7.10 | all-reduce | flops 32768 | bytes 196608 | tf_op jit(solution)/shard_map/psum | solution.py:36
  157.8 1.3 convolution_add_fusion.1
  159.1 2.0 convolution_bitcast_fusion
  161.9 1.6 copy.27
  164.3 29.7 %all-reduce.14.cloned.1.call-done = f32[1,128,128]{1,2,0:T(8,128)} async-done(((f32[1,128,128]{1,2,0:T(8,128)}), f32[1,128,128]{1,2,0:T(8,128)}) %all-reduce.14.cloned.1.call-update) | async-done | bytes 65552 | tf_op jit(solution)/shard_map/psum | solution.py:47
  195.8 11.7 %custom-call.11 = f32[1,128,128]{2,1,0:T(8,128)S(1)} custom-call(f32[1,128,128]{2,1,0:T(8,128)S(1)} %fusion.41), custom_call_target="Cholesky" | custom-call | tf_op jit(solution)/shard_map/jit(cholesky)/cholesky | solution.py:48
  208.9 9.8 %custom-call.12 = f32[1,1,128,128]{2,3,1,0:T(8,128)S(1)} custom-call(f32[1,1,128,128]{3,2,1,0:T(8,128)S(1)} %fusion.39), custom_call_target="InvertDiagBlocksLowerTriangular" | custom-call | tf_op jit(solution)/shard_map/vmap(jit(_solve_triangular))/triangular_solve | solution.py:26
  220.5 1.2 convolution_bitcast_fusion.3
  223.0 2.2 convolution_bitcast_fusion.2
  225.2 20.2 %all-reduce.20 = (bf16[1,128,128]{2,1,0:T(8,128)(2,1)S(1)}, bf16[1,128,128]{2,1,0:T(8,128)(2,1)S(1)}) all-reduce(f32[1,128,128]{2,1,0:T(8,128)} %convolution_bitcast_fusion.3, f32[1,128,128]{2,1,0:T(8,128)} %convolution_bitcast_fusion.2), channel_id=1, replica_groups=mesh['leaf'=8,'front'=4] {'front'}, use_global_device_ids=true, to_apply=%region_10.13 | all-reduce | flops 32768 | bytes 196608 | tf_op jit(solution)/shard_map/psum | solution.py:56
  247.2 15.8 %psum.95 = f32[64,128]{1,0:T(8,128)S(1)} all-reduce(f32[64,128]{1,0:T(8,128)S(1)} %fusion.63), channel_id=1, replica_groups=mesh['leaf'=8,'front'=4] {'front'}, use_global_device_ids=true, to_apply=%region_13.16 | all-reduce | flops 8192 | bytes 65536 | tf_op jit(solution)/shard_map/psum | solution.py:105
  263.0 16.4 %all-reduce.16.cloned.1.call-done = f32[128,128]{1,0:T(8,128)} async-done(((f32[128,128]{1,0:T(8,128)}), f32[128,128]{1,0:T(8,128)}) %all-reduce.16.cloned.1.call-update) | async-done | bytes 65552 | tf_op jit(solution)/shard_map/psum | solution.py:105
  279.4 58.2 %while.13 = (s32[]{:T(128)}, f32[64,128]{1,0:T(8,128)S(1)}, f32[64,128]{1,0:T(8,128)}, f32[128,128]{1,0:T(8,128)}, f32[64,128]{1,0:T(8,128)S(1)}, /*index=5*/s32[]{:T(128)}, s32[]{:T(128)}) while((s32[]{:T(128)}, f32[64,128]{1,0:T(8,128)S(1)}, f32[64,128]{1,0:T(8,128)}, f32[128,128]{1,0:T(8,128)}, f32[64,128]{1,0:T(8,128)S(1)}, ...), condition=%wide.region_15.18_spmd.clone, body=%wide.region_14.17_spmd.clone.sunk | while | flops 12599299 | bytes 491675 | solution.py:115
  279.5 1.9 collective-permute-start
  281.4 4.2 %collective-permute-done = f32[64,128]{1,0:T(8,128)S(1)} collective-permute-done((f32[64,128]{1,0:T(8,128)S(1)}, f32[64,128]{1,0:T(8,128)S(1)}, u32[]{:S(2)}, u32[]{:S(2)}) %collective-permute-start) | collective-permute-done | bytes 32800 | tf_op jit(solution)/shard_map/while/body/eval_jaxpr/ppermute | solution.py:14
  285.6 1.1 convolution_subtract_fusion.3
  286.7 1.9 collective-permute-start
  288.7 4.2 %collective-permute-done = f32[64,128]{1,0:T(8,128)S(1)} collective-permute-done((f32[64,128]{1,0:T(8,128)S(1)}, f32[64,128]{1,0:T(8,128)S(1)}, u32[]{:S(2)}, u32[]{:S(2)}) %collective-permute-start) | collective-permute-done | bytes 32800 | tf_op jit(solution)/shard_map/while/body/eval_jaxpr/ppermute | solution.py:14
  292.9 1.1 convolution_subtract_fusion.3
  294.0 1.9 collective-permute-start
  295.9 4.2 %collective-permute-done = f32[64,128]{1,0:T(8,128)S(1)} collective-permute-done((f32[64,128]{1,0:T(8,128)S(1)}, f32[64,128]{1,0:T(8,128)S(1)}, u32[]{:S(2)}, u32[]{:S(2)}) %collective-permute-start) | collective-permute-done | bytes 32800 | tf_op jit(solution)/shard_map/while/body/eval_jaxpr/ppermute | solution.py:14
  301.3 1.9 collective-permute-start
  303.2 4.2 %collective-permute-done = f32[64,128]{1,0:T(8,128)S(1)} collective-permute-done((f32[64,128]{1,0:T(8,128)S(1)}, f32[64,128]{1,0:T(8,128)S(1)}, u32[]{:S(2)}, u32[]{:S(2)}) %collective-permute-start) | collective-permute-done | bytes 32800 | tf_op jit(solution)/shard_map/while/body/eval_jaxpr/ppermute | solution.py:14
  308.5 1.9 collective-permute-start
  310.5 4.2 %collective-permute-done = f32[64,128]{1,0:T(8,128)S(1)} collective-permute-done((f32[64,128]{1,0:T(8,128)S(1)}, f32[64,128]{1,0:T(8,128)S(1)}, u32[]{:S(2)}, u32[]{:S(2)}) %collective-permute-start) | collective-permute-done | bytes 32800 | tf_op jit(solution)/shard_map/while/body/eval_jaxpr/ppermute | solution.py:14
  315.8 1.9 collective-permute-start
  317.8 4.2 %collective-permute-done = f32[64,128]{1,0:T(8,128)S(1)} collective-permute-done((f32[64,128]{1,0:T(8,128)S(1)}, f32[64,128]{1,0:T(8,128)S(1)}, u32[]{:S(2)}, u32[]{:S(2)}) %collective-permute-start) | collective-permute-done | bytes 32800 | tf_op jit(solution)/shard_map/while/body/eval_jaxpr/ppermute | solution.py:14
  323.1 1.9 collective-permute-start
  325.0 4.2 %collective-permute-done = f32[64,128]{1,0:T(8,128)S(1)} collective-permute-done((f32[64,128]{1,0:T(8,128)S(1)}, f32[64,128]{1,0:T(8,128)S(1)}, u32[]{:S(2)}, u32[]{:S(2)}) %collective-permute-start) | collective-permute-done | bytes 32800 | tf_op jit(solution)/shard_map/while/body/eval_jaxpr/ppermute | solution.py:14
  329.2 1.1 convolution_subtract_fusion.3
  330.4 1.9 collective-permute-start
  332.3 4.2 %collective-permute-done = f32[64,128]{1,0:T(8,128)S(1)} collective-permute-done((f32[64,128]{1,0:T(8,128)S(1)}, f32[64,128]{1,0:T(8,128)S(1)}, u32[]{:S(2)}, u32[]{:S(2)}) %collective-permute-start) | collective-permute-done | bytes 32800 | tf_op jit(solution)/shard_map/while/body/eval_jaxpr/ppermute | solution.py:14
  337.6 2.0 fusion.2
  (117 shorter events, 27.9 us)
Async XLA Ops:
  6.5 31.6 %copy-start = (bf16[1,3,512,512]{3,2,1,0:T(8,128)(2,1)S(1)}, bf16[1,3,512,512]{3,2,1,0:T(8,128)(2,1)}, u32[]{:S(2)}) copy-start(bf16[1,3,512,512]{3,2,1,0:T(8,128)(2,1)} %param.15) | copy-start | bytes 4718596
  6.5 4.9 %copy-start.3 = (bf16[1536,128]{1,0:T(8,128)(2,1)S(1)}, bf16[1536,128]{1,0:T(8,128)(2,1)}, u32[]{:S(2)}) copy-start(bf16[1536,128]{1,0:T(8,128)(2,1)} %param.14) | copy-start | bytes 1179652
  6.5 4.1 %copy-start.20 = (bf16[1,64,1536]{2,1,0:T(8,128)(2,1)S(1)}, bf16[1,64,1536]{2,1,0:T(8,128)(2,1)}, u32[]{:S(2)}) copy-start(bf16[1,64,1536]{2,1,0:T(8,128)(2,1)} %param.16) | copy-start | bytes 589828
  6.5 63.9 %all-reduce.12.cloned.1.call-start = ((), (), s32[]{:S(2)}) async-start(), calls=%async_computation | async-start | bytes 131072 | tf_op jit(solution)/shard_map/psum | solution.py:47
  6.5 4.9 %collective-permute-start.2 = (bf16[1,1536,128]{2,1,0:T(8,128)(2,1)}, bf16[1,1536,128]{2,1,0:T(8,128)(2,1)S(1)}, u32[]{:S(2)}, u32[]{:S(2)}) collective-permute-start(bf16[1,1536,128]{2,1,0:T(8,128)(2,1)} %param.12), channel_id=1, source_target_pairs={{0,4},{4,0},{8,12},{12,8},{16,20},{20,16},{24,28},{28,24},{1,5},{5... | collective-permute-start | bytes 1179656 | tf_op jit(solution)/shard_map/ppermute | solution.py:8
  8.8 25.1 %copy-start.4 = (bf16[1,1536,128]{2,1,0:T(8,128)(2,1)}, bf16[1,1536,128]{2,1,0:T(8,128)(2,1)S(1)}, u32[]{:S(2)}) copy-start(bf16[1,1536,128]{2,1,0:T(8,128)(2,1)S(1)} %fusion.17) | copy-start | bytes 1179652
  8.8 25.1 %collective-permute-start.1 = (bf16[1,1536,128]{2,1,0:T(8,128)(2,1)S(1)}, bf16[1,1536,128]{2,1,0:T(8,128)(2,1)S(1)}, u32[]{:S(2)}, u32[]{:S(2)}) collective-permute-start(bf16[1,1536,128]{2,1,0:T(8,128)(2,1)S(1)} %fusion.17), channel_id=1, source_target_pairs={{0,4},{4,0},{8,12},{12,8},{16,20},{20,16},{24,28},{28,24},{1,5},{5... | collective-permute-start | bytes 1179656 | tf_op jit(solution)/shard_map/ppermute | solution.py:8
  11.5 24.5 %copy-start.12 = (bf16[1,1536,128]{2,1,0:T(8,128)(2,1)}, bf16[1,1536,128]{2,1,0:T(8,128)(2,1)S(1)}, u32[]{:S(2)}) copy-start(bf16[1,1536,128]{2,1,0:T(8,128)(2,1)S(1)} %collective-permute-done.2) | copy-start | bytes 1179652
  33.9 0.8 copy-start.15
  34.7 3.4 copy-start.18
  38.0 156.0 %all-reduce.14.cloned.1.call-start = ((), (), s32[]{:S(2)}) async-start(), calls=%async_computation.1 | async-start | bytes 131072 | tf_op jit(solution)/shard_map/psum | solution.py:47
  97.4 25.4 %copy-start.9 = (bf16[1,1536,128]{2,1,0:T(8,128)(2,1)S(1)}, bf16[1,1536,128]{2,1,0:T(8,128)(2,1)}, u32[]{:S(2)}) copy-start(bf16[1,1536,128]{2,1,0:T(8,128)(2,1)} %param.12) | copy-start | bytes 1179652
  99.7 24.2 %copy-start.13 = (bf16[1,1536,128]{2,1,0:T(8,128)(2,1)S(1)}, bf16[1,1536,128]{2,1,0:T(8,128)(2,1)}, u32[]{:S(2)}) copy-start(bf16[1,1536,128]{2,1,0:T(8,128)(2,1)} %copy-done.12) | copy-start | bytes 1179652
  124.9 0.9 copy-start.5
  125.8 10.1 %collective-permute-start.4 = (bf16[1,1536,128]{1,2,0:T(8,128)(2,1)S(1)}, bf16[1,1536,128]{1,2,0:T(8,128)(2,1)S(1)}, u32[]{:S(2)}, u32[]{:S(2)}) collective-permute-start(bf16[1,1536,128]{1,2,0:T(8,128)(2,1)S(1)} %bitcast.187), channel_id=1, source_target_pairs={{0,8},{4,12},{8,0},{12,4},{16,24},{20,28},{24,16},{28,20},{1,9},{5... | collective-permute-start | bytes 1179656 | tf_op jit(solution)/shard_map/ppermute | solution.py:8
  127.3 29.7 %collective-permute-start.3 = (bf16[1,1536,128]{1,2,0:T(8,128)(2,1)S(1)}, bf16[1,1536,128]{1,2,0:T(8,128)(2,1)S(1)}, u32[]{:S(2)}, u32[]{:S(2)}) collective-permute-start(bf16[1,1536,128]{1,2,0:T(8,128)(2,1)S(1)} %fusion.61), channel_id=1, source_target_pairs={{0,8},{4,12},{8,0},{12,4},{16,24},{20,28},{24,16},{28,20},{1,9},{5... | collective-permute-start | bytes 1179656 | tf_op jit(solution)/shard_map/ppermute | solution.py:8
  135.9 0.8 copy-start.10
  156.7 1.1 copy-start.21
  157.0 0.7 copy-start.14
  157.8 3.5 copy-start.7
  161.2 118.3 %all-reduce.16.cloned.1.call-start = ((), (), s32[]{:S(2)}) async-start(), calls=%async_computation.2 | async-start | bytes 131072 | tf_op jit(solution)/shard_map/psum | solution.py:105
  219.6 0.9 copy-start.1
  221.9 1.1 copy-start.2
  222.5 22.9 %copy-start.6 = (bf16[128,1536]{1,0:T(8,128)(2,1)S(1)}, bf16[128,1536]{1,0:T(8,128)(2,1)}, u32[]{:S(2)}) copy-start(bf16[128,1536]{1,0:T(8,128)(2,1)} %copy-done.5) | copy-start | bytes 1179652
  223.0 22.7 %copy-start.11 = (bf16[1,1536,128]{1,2,0:T(8,128)(2,1)S(1)}, bf16[1,1536,128]{1,2,0:T(8,128)(2,1)}, u32[]{:S(2)}) copy-start(bf16[1,1536,128]{1,2,0:T(8,128)(2,1)} %copy-done.10) | copy-start | bytes 1179652
  245.4 1.6 copy-start.19
  245.7 33.7 %copy-start.17 = (f32[64,128]{1,0:T(8,128)S(1)}, f32[64,128]{1,0:T(8,128)}, u32[]{:S(2)}) copy-start(f32[64,128]{1,0:T(8,128)} %custom-call.8) | copy-start | bytes 98308
  246.1 91.6 %copy-start.8 = (f32[3,8,8,512]{3,2,0,1:T(8,128)S(1)}, f32[3,8,8,512]{3,2,0,1:T(8,128)}, u32[]{:S(2)}) copy-start(f32[3,8,8,512]{3,2,0,1:T(8,128)} %copy.26) | copy-start | bytes 1179652
  279.5 6.1 %collective-permute-start = (f32[64,128]{1,0:T(8,128)S(1)}, f32[64,128]{1,0:T(8,128)S(1)}, u32[]{:S(2)}, u32[]{:S(2)}) collective-permute-start(f32[64,128]{1,0:T(8,128)S(1)} %broadcast_select_fusion.2), channel_id=1, source_target_pairs={{0,4},{4,8},{8,12},{12,16},{16,20},{20,24},{24,28},{1,5},{5,9},{9,... | collective-permute-start | bytes 98312 | tf_op jit(solution)/shard_map/while/body/eval_jaxpr/ppermute | solution.py:14
  285.6 1.1 copy-start.16
  286.7 6.1 %collective-permute-start = (f32[64,128]{1,0:T(8,128)S(1)}, f32[64,128]{1,0:T(8,128)S(1)}, u32[]{:S(2)}, u32[]{:S(2)}) collective-permute-start(f32[64,128]{1,0:T(8,128)S(1)} %broadcast_select_fusion.2), channel_id=1, source_target_pairs={{0,4},{4,8},{8,12},{12,16},{16,20},{20,24},{24,28},{1,5},{5,9},{9,... | collective-permute-start | bytes 98312 | tf_op jit(solution)/shard_map/while/body/eval_jaxpr/ppermute | solution.py:14
  292.9 1.1 copy-start.16
  294.0 6.1 %collective-permute-start = (f32[64,128]{1,0:T(8,128)S(1)}, f32[64,128]{1,0:T(8,128)S(1)}, u32[]{:S(2)}, u32[]{:S(2)}) collective-permute-start(f32[64,128]{1,0:T(8,128)S(1)} %broadcast_select_fusion.2), channel_id=1, source_target_pairs={{0,4},{4,8},{8,12},{12,16},{16,20},{20,24},{24,28},{1,5},{5,9},{9,... | collective-permute-start | bytes 98312 | tf_op jit(solution)/shard_map/while/body/eval_jaxpr/ppermute | solution.py:14
  300.1 1.1 copy-start.16
  301.3 6.1 %collective-permute-start = (f32[64,128]{1,0:T(8,128)S(1)}, f32[64,128]{1,0:T(8,128)S(1)}, u32[]{:S(2)}, u32[]{:S(2)}) collective-permute-start(f32[64,128]{1,0:T(8,128)S(1)} %broadcast_select_fusion.2), channel_id=1, source_target_pairs={{0,4},{4,8},{8,12},{12,16},{16,20},{20,24},{24,28},{1,5},{5,9},{9,... | collective-permute-start | bytes 98312 | tf_op jit(solution)/shard_map/while/body/eval_jaxpr/ppermute | solution.py:14
  307.4 1.1 copy-start.16
  308.5 6.1 %collective-permute-start = (f32[64,128]{1,0:T(8,128)S(1)}, f32[64,128]{1,0:T(8,128)S(1)}, u32[]{:S(2)}, u32[]{:S(2)}) collective-permute-start(f32[64,128]{1,0:T(8,128)S(1)} %broadcast_select_fusion.2), channel_id=1, source_target_pairs={{0,4},{4,8},{8,12},{12,16},{16,20},{20,24},{24,28},{1,5},{5,9},{9,... | collective-permute-start | bytes 98312 | tf_op jit(solution)/shard_map/while/body/eval_jaxpr/ppermute | solution.py:14
  314.7 1.1 copy-start.16
  315.8 6.1 %collective-permute-start = (f32[64,128]{1,0:T(8,128)S(1)}, f32[64,128]{1,0:T(8,128)S(1)}, u32[]{:S(2)}, u32[]{:S(2)}) collective-permute-start(f32[64,128]{1,0:T(8,128)S(1)} %broadcast_select_fusion.2), channel_id=1, source_target_pairs={{0,4},{4,8},{8,12},{12,16},{16,20},{20,24},{24,28},{1,5},{5,9},{9,... | collective-permute-start | bytes 98312 | tf_op jit(solution)/shard_map/while/body/eval_jaxpr/ppermute | solution.py:14
  322.0 1.1 copy-start.16
  323.1 6.1 %collective-permute-start = (f32[64,128]{1,0:T(8,128)S(1)}, f32[64,128]{1,0:T(8,128)S(1)}, u32[]{:S(2)}, u32[]{:S(2)}) collective-permute-start(f32[64,128]{1,0:T(8,128)S(1)} %broadcast_select_fusion.2), channel_id=1, source_target_pairs={{0,4},{4,8},{8,12},{12,16},{16,20},{20,24},{24,28},{1,5},{5,9},{9,... | collective-permute-start | bytes 98312 | tf_op jit(solution)/shard_map/while/body/eval_jaxpr/ppermute | solution.py:14
  329.2 1.1 copy-start.16
  330.4 6.1 %collective-permute-start = (f32[64,128]{1,0:T(8,128)S(1)}, f32[64,128]{1,0:T(8,128)S(1)}, u32[]{:S(2)}, u32[]{:S(2)}) collective-permute-start(f32[64,128]{1,0:T(8,128)S(1)} %broadcast_select_fusion.2), channel_id=1, source_target_pairs={{0,4},{4,8},{8,12},{12,16},{16,20},{20,24},{24,28},{1,5},{5,9},{9,... | collective-permute-start | bytes 98312 | tf_op jit(solution)/shard_map/while/body/eval_jaxpr/ppermute | solution.py:14
  336.5 1.1 copy-start.16
Sparse Core Ops, SparseCore 0:
  38.2 32.2 all-reduce.11
  161.3 32.6 all-reduce.13
  247.1 32.2 all-reduce.15
where the time goes:
time: 348 us; the launch traced here: 346 us
  waiting for transfers between devices  119 us (34%)
  blocking collectives  98 us (28%)
  other arithmetic  50.1 us (14%)
  matrix products  37.7 us (11%)
  starting transfers between devices  18 us (5%)
  between operations  13.5 us (4%)
  local copies, waits for them, and re-layouts  9.82 us (3%)
    psum x2, waiting for transfers between devices, merge_pairs(): gram = lax.psum(gram_local, 'front')  60.7 us
    psum x2, blocking collectives, merge_pairs(): lax.psum((weight_first, second_weight), 'front')  41.1 us
    psum x2, blocking collectives, merge_pairs(): proj_first, proj_second = lax.psum((proj_first, proj_second), 'front')  41 us
    ppermute x8, waiting for transfers between devices, passed_along(): lax.ppermute(value, axis, [(source, source + steps) for source in range(f...  33.6 us
    another operation x6, other arithmetic, merge_pairs(): factor = jnp.linalg.cholesky(gram)  24.8 us
    another operation x4, other arithmetic, right_solve(): jax.scipy.linalg.solve_triangular(factor_one, block_one.T, lower=True)  21.5 us
    psum x1, waiting for transfers between devices, on_device(): matrix, vector = lax.psum((matrix_local, vector_local), 'front')  16.4 us
    psum x1, blocking collectives, on_device(): matrix, vector = lax.psum((matrix_local, vector_local), 'front')  15.8 us
  transfers between devices with their start and end apart: 15, of which 12 were waited for; matrix products, arithmetic and copies ran while one was open for 3% of the time, Pallas kernels for 0%

commit v1 on v0

v1 whole, which is shorter than its diff:
```python
import functools

import jax
import jax.numpy as jnp
from jax import lax
from jax.experimental import pallas as pl
from jax.experimental.pallas import tpu as pltpu
from jax.sharding import PartitionSpec as P

MESH = pl.DeviceIdType.MESH
F32 = jnp.float32
BF16 = jnp.bfloat16
PANEL = 8


def dot(a, b):
    return jnp.dot(a, b, preferred_element_type=F32)


def dot_nt(a, b):
    return lax.dot_general(a, b, (((1,), (1,)), ((), ())), preferred_element_type=F32)


def dot_tn(a, b):
    return lax.dot_general(a, b, (((0,), (0,)), ((), ())), preferred_element_type=F32)


def full(a, b, ca=1, cb=0):
    return lax.dot_general(
        a,
        b,
        (((ca,), (cb,)), ((), ())),
        precision=lax.Precision.HIGHEST,
        preferred_element_type=F32,
    )


def halves(x):
    high = x.astype(BF16)
    return high, (x - high.astype(F32)).astype(BF16)


def flip(index, bit):
    return index + bit - 2 * bit * lax.rem(index // bit, 2)


def inverse_factors(grams, work, inverse):
    size = grams[0].shape[0]
    eye = (
        lax.broadcasted_iota(jnp.int32, (size, size), 0)
        == lax.broadcasted_iota(jnp.int32, (size, size), 1)
    ).astype(F32)
    for q, gram in enumerate(grams):
        work[q, :, :size] = gram
        work[q, :, size:] = eye
    lane = lax.broadcasted_iota(jnp.int32, (PANEL, size), 1)
    row = lax.broadcasted_iota(jnp.int32, (PANEL, size), 0)

    def step(b, carry):
        base = pl.multiple_of(b * PANEL, PANEL)
        for q in range(len(grams)):
            left = work[q, pl.ds(base, PANEL), :size]
            right = work[q, pl.ds(base, PANEL), size:]
            columns = [
                jnp.broadcast_to(
                    jnp.sum(jnp.where(lane == base + j, left, 0.0), axis=1, keepdims=True),
                    (PANEL, size),
                )
                for j in range(PANEL)
            ]
            pivots = jnp.zeros((PANEL, size), F32)
            for j in range(PANEL):
                pivots = jnp.where(row == j, columns[j], pivots)
                times = jnp.where(row > j, columns[j] * (1.0 / columns[j][j : j + 1, :]), 0.0)
                left = left - times * left[j : j + 1, :]
                right = right - times * right[j : j + 1, :]
                for k in range(j + 1, PANEL):
                    columns[k] = columns[k] - times * columns[k][j : j + 1, :]
            scale = lax.rsqrt(pivots)
            scale = scale * (1.5 - 0.5 * pivots * scale * scale)
            left = left * scale
            right = right * scale
            inverse[q, pl.ds(base, PANEL), :] = right
            below = jnp.where(lane >= base + PANEL, left, 0.0)
            work[q] -= full(below, jnp.concatenate([left, right], axis=1), 0, 0)
        return carry

    lax.fori_loop(0, size // PANEL, step, 0)


def kernel(
    leaves, fronts, rank_ref, u_ref, v_ref, sketch_ref, dinv_ref, rhs_ref, out_ref,
    uall, vall, strip, landed, gath, work, inverse, wide, part, landed2, whole, hyper, sol,
    a_send, a_recv, rs_send, rs_recv, ag_send, ag_recv, d_send, d_recv,
    rs2_send, rs2_recv, ag2_send, ag2_recv, h_send, h_recv,
):
    leaf = lax.axis_index("leaf")
    front = lax.axis_index("front")
    tiles, tile = dinv_ref.shape[1], dinv_ref.shape[2]
    rank = u_ref.shape[2]
    sides = rhs_ref.shape[1]
    levels = leaves.bit_length() - 1
    mine = lax.rem(leaf, 4)
    sibling, cousin = flip(leaf, 1), flip(leaf, 2)
    theirs, across = flip(mine, 1), flip(mine, 2)
    opposite = flip(theirs, 2)
    shard = strip.shape[0] // fronts
    shard2 = part.shape[0] // fronts

    barrier = pltpu.get_barrier_semaphore()
    for level in range(levels):
        pl.semaphore_signal(barrier, inc=1, device_id=(flip(leaf, 1 << level), front), device_id_type=MESH)
    for d in range(1, fronts):
        pl.semaphore_signal(barrier, inc=1, device_id=(leaf, lax.rem(front + d, fronts)), device_id_type=MESH)

    def rows(t):
        return pl.ds(t * tile, tile)

    column = lax.broadcasted_iota(jnp.int32, (tile, rank), 1)
    for t in range(tiles):
        keep = column < rank_ref[0, t]
        uall[mine, rows(t), :] = jnp.where(keep, u_ref[0, rows(t), :].astype(F32), 0.0).astype(BF16)
        vall[mine, rows(t), :] = v_ref[0, rows(t), :]
    pl.semaphore_wait(barrier, levels + fronts - 1)

    def remote(src, dst, send, recv, target):
        return pltpu.make_async_remote_copy(
            src_ref=src, dst_ref=dst, send_sem=send, recv_sem=recv, device_id=target, device_id_type=MESH
        )

    def factor_copy(kind, path, t):
        held = (uall, vall)[kind]
        block = held.at[across if path == 2 else mine, rows(t), :]
        target = (cousin if path == 1 else sibling, front)
        return remote(block, block, a_send.at[kind, path, t], a_recv.at[kind, path, t], target)

    for kind in range(2):
        for path in (1, 0):
            for t in range(tiles):
                factor_copy(kind, path, t).start()

    def scatter_copy(f, buffer, landing, size, send, recv):
        return remote(buffer.at[pl.ds(f * size, size), :], landing.at[front], send.at[f], recv.at[front], (leaf, f))

    def landing_wait(s, buffer, landing, size, send, recv):
        remote(buffer.at[pl.ds(0, size), :], landing.at[s], send.at[s], recv.at[s], (leaf, s)).wait_recv()

    first = (strip, landed, shard, rs_send, rs_recv)
    second = (part, landed2, shard2, rs2_send, rs2_recv)

    def scatter(lower, upper, what):
        for f in range(lower, upper):
            @pl.when(front != f)
            def _(f=f):
                scatter_copy(f, *what).start()

    own_t = uall[mine].T
    strip[pl.ds(0, rank), :] = dot_tn(vall[mine], sketch_ref[...])
    scatter(0, fronts // 4, first)
    strip[pl.ds(rank, rank), :] = dot(own_t, uall[mine])
    scatter(fronts // 4, fronts // 2, first)

    for t in range(tiles):
        sol[:, rows(t)] = dot_nt(rhs_ref[0, :, rows(t)], dinv_ref[0, t])

    for t in range(tiles):
        factor_copy(0, 1, t).wait_recv()
        factor_copy(0, 2, t).start()
    for t in range(tiles):
        factor_copy(0, 0, t).wait_recv()
    for t in range(tiles):
        factor_copy(0, 2, t).wait_recv()
    for j in (1, 2):
        strip[pl.ds((j + 1) * rank, rank), :] = dot(own_t, uall[lax.rem(mine + j, 4)])
        scatter((j + 1) * fronts // 4, (j + 2) * fronts // 4, first)

    def reduced(buffer, landing, size, send, recv):
        total = buffer[pl.ds(pl.multiple_of(front * size, 8), size), :]
        for s in range(fronts):
            @pl.when(front != s)
            def _(s=s):
                landing_wait(s, buffer, landing, size, send, recv)

            total = total + jnp.where(front != s, landing[s], 0.0)
        return total

    for s in range(fronts):
        @pl.when(front == s)
        def _(s=s):
            landed[s] = jnp.zeros(landed.shape[1:], F32)
            landed2[s] = jnp.zeros(landed2.shape[1:], F32)

    def piece(i, s):
        return gath.at[i, pl.ds(s * shard, shard), :]

    def gather_copy(d):
        return remote(
            piece(mine, front), piece(mine, front), ag_send.at[d], ag_recv.at[d], (leaf, lax.rem(front + d, fronts))
        )

    def spread_copy(path, d):
        block = piece(across if path == 2 else mine, lax.rem(front - d + fronts, fronts))
        target = (cousin if path == 1 else sibling, front)
        return remote(block, block, d_send.at[path, d], d_recv.at[path, d], target)

    gath[mine, pl.ds(pl.multiple_of(front * shard, 8), shard), :] = reduced(*first)
    for d in range(1, fronts):
        gather_copy(d).start()
    for d in range(fronts):
        if d:
            gather_copy(d).wait_recv()
        spread_copy(1, d).start()
        spread_copy(0, d).start()
    for t in range(tiles):
        factor_copy(1, 1, t).wait_recv()
        factor_copy(1, 2, t).start()
    for d in range(fronts):
        spread_copy(1, d).wait_recv()
        spread_copy(2, d).start()
    for d in range(fronts):
        spread_copy(0, d).wait_recv()
    for d in range(fronts):
        spread_copy(2, d).wait_recv()

    def block(i, j):
        return gath[i, pl.ds(j * rank, rank), :]

    def square(a, b, c, d):
        wide[pl.ds(0, rank), pl.ds(0, rank)] = a
        wide[pl.ds(0, rank), pl.ds(rank, rank)] = b
        wide[pl.ds(rank, rank), pl.ds(0, rank)] = c
        wide[pl.ds(rank, rank), pl.ds(rank, rank)] = d
        return wide[...]

    raw, small, cross, grams = [], [], [], []
    for p in range(2):
        a, b = 2 * p, 2 * p + 1
        between = block(a, 2)
        pair = square(block(a, 1), between, between.T, block(b, 1))
        raw.append(jnp.concatenate([block(a, 0), block(b, 0)], axis=0))
        small.append(raw[p].astype(BF16).astype(F32))
        cross.append(full(pair, small[p]))
        grams.append(full(small[p], cross[p], 0, 0))
    inverse_factors(grams, work, inverse)
    turn = [full(small[p], inverse[p], 1, 1) for p in range(2)]
    weight = [full(cross[p], inverse[p], 1, 1).astype(BF16).astype(F32) for p in range(2)]
    small2 = [full(weight[p], raw[p], 0, 0).astype(BF16).astype(F32) for p in range(2)]
    pair = square(block(0, 3), block(3, 2).T, block(1, 2), block(1, 3))
    middle = full(turn[0], full(pair, turn[1]), 0, 0)
    cross2 = [small2[0] + full(middle, small2[1]), full(middle, small2[0], 0, 0) + small2[1]]
    gram2 = full(small2[0], cross2[0], 0, 0) + full(small2[1], cross2[1], 0, 0)
    inverse_factors([gram2], work, inverse)
    turn2 = [halves(full(turn[p], full(small2[p], inverse[0], 1, 1))) for p in range(2)]
    weight2 = [
        halves(full(weight[p], full(cross2[p], inverse[0], 1, 1).astype(BF16).astype(F32))) for p in range(2)
    ]

    def combined(held, factors):
        total = None
        for i in range(4):
            half = slice((i % 2) * rank, (i % 2 + 1) * rank)
            for part_of in factors[i // 2]:
                term = dot(held[i], part_of[half])
                total = term if total is None else total + term
        return total.astype(BF16)

    left_f = combined(uall, turn2)
    coupled = [dot(dinv_ref[0, t], left_f[t * tile : (t + 1) * tile]).astype(BF16) for t in range(tiles)]
    for path in (0, 2):
        for t in range(tiles):
            factor_copy(1, path, t).wait_recv()
    right_f = combined(vall, weight2)
    used = rank + sides
    if used < part.shape[0]:
        part[pl.ds(used, part.shape[0] - used), :] = jnp.zeros((part.shape[0] - used, rank), F32)
    part[pl.ds(0, rank), :] = -dot_tn(jnp.concatenate(coupled, axis=0), right_f)
    part[pl.ds(rank, sides), :] = dot(sol[...].astype(BF16), right_f)

    scatter(0, fronts, second)

    def piece2(s):
        return whole.at[pl.ds(s * shard2, shard2), :]

    def gather2_copy(d):
        return remote(
            piece2(front), piece2(front), ag2_send.at[d], ag2_recv.at[d], (leaf, lax.rem(front + d, fronts))
        )

    whole[pl.ds(pl.multiple_of(front * shard2, 8), shard2), :] = reduced(*second)
    for d in range(1, fronts):
        gather2_copy(d).start()
    for d in range(1, fronts):
        gather2_copy(d).wait_recv()

    hyper[0, 0] = whole[pl.ds(0, used), :]
    low = lax.broadcasted_iota(jnp.int32, (used, rank), 0)
    along = lax.broadcasted_iota(jnp.int32, (used, rank), 1)
    prefix = jnp.where(low == along, 1.0, 0.0)

    def then(first_map, second_map):
        return full(first_map, second_map[:rank]) + jnp.where(low >= rank, second_map, 0.0)

    def hyper_copy(k):
        send = pl.ds(0, used) if k < levels - 1 else pl.ds(rank, sides)
        return remote(
            hyper.at[k, 0, send, :], hyper.at[k, 1, send, :], h_send.at[k], h_recv.at[k], (flip(leaf, 1 << k), front)
        )

    previous = None
    for k in range(levels):
        hyper_copy(k).start()
        hyper_copy(k).wait_recv()
        upper = lax.rem(leaf // (1 << k), 2) == 1
        if k < levels - 1:
            here, there = hyper[k, 0], hyper[k, 1]
            hyper[k + 1, 0] = then(jnp.where(upper, there, here), jnp.where(upper, here, there))
            prefix = jnp.where(upper, then(there, prefix), prefix)
        else:
            there = hyper[k, 1, pl.ds(rank, sides), :]
            previous = prefix[rank:] + jnp.where(upper, full(there, prefix[:rank]), 0.0)

    for t in range(tiles):
        total = sol[:, rows(t)]
        for part_of in halves(previous):
            total = total - dot_nt(part_of, coupled[t])
        out_ref[0, :, rows(t)] = total

    for kind in range(2):
        for path in range(3):
            for t in range(tiles):
                factor_copy(kind, path, t).wait_send()
    for f in range(fronts):
        @pl.when(front != f)
        def _(f=f):
            scatter_copy(f, *first).wait_send()
            scatter_copy(f, *second).wait_send()
    for d in range(1, fronts):
        gather_copy(d).wait_send()
        gather2_copy(d).wait_send()
    for path in range(3):
        for d in range(fronts):
            spread_copy(path, d).wait_send()
    for k in range(levels):
        hyper_copy(k).wait_send()


def solution(mesh):
    leaves, fronts = mesh.shape["leaf"], mesh.shape["front"]
    levels = leaves.bit_length() - 1

    def on_device(child_left_factors, child_v, ranks, sketch, dinv, rhs):
        _, length, rank = child_left_factors.shape
        tiles = dinv.shape[1]
        sides = rhs.shape[1]
        used = rank + sides
        shard = 4 * rank // fronts
        shard2 = -(-used // (8 * fronts)) * 8
        vmem = pl.BlockSpec(memory_space=pltpu.VMEM)
        dma = pltpu.SemaphoreType.DMA
        return pl.pallas_call(
            functools.partial(kernel, leaves, fronts),
            out_shape=jax.ShapeDtypeStruct((1, sides, length), F32),
            in_specs=[pl.BlockSpec(memory_space=pltpu.SMEM)] + [vmem] * 5,
            out_specs=vmem,
            scratch_shapes=[
                pltpu.VMEM((4, length, rank), BF16),
                pltpu.VMEM((4, length, rank), BF16),
                pltpu.VMEM((4 * rank, rank), F32),
                pltpu.VMEM((fronts, shard, rank), F32),
                pltpu.VMEM((4, 4 * rank, rank), F32),
                pltpu.VMEM((2, rank, 2 * rank), F32),
                pltpu.VMEM((2, rank, rank), F32),
                pltpu.VMEM((2 * rank, 2 * rank), F32),
                pltpu.VMEM((shard2 * fronts, rank), F32),
                pltpu.VMEM((fronts, shard2, rank), F32),
                pltpu.VMEM((shard2 * fronts, rank), F32),
                pltpu.VMEM((levels, 2, used, rank), F32),
                pltpu.VMEM((sides, length), F32),
                dma((2, 3, tiles)),
                dma((2, 3, tiles)),
                dma((fronts,)),
                dma((fronts,)),
                dma((fronts,)),
                dma((fronts,)),
                dma((3, fronts)),
                dma((3, fronts)),
                dma((fronts,)),
                dma((fronts,)),
                dma((fronts,)),
                dma((fronts,)),
                dma((levels,)),
                dma((levels,)),
            ],
            compiler_params=pltpu.CompilerParams(
                collective_id=0, has_side_effects=True, vmem_limit_bytes=40 * 1024 * 1024
            ),
        )(ranks, child_left_factors, child_v, sketch, dinv, rhs)

    placed = (
        P("leaf", "front", None),
        P("leaf", "front", None),
        P("leaf", "front"),
        P("front", None),
        P("leaf", "front", None, None),
        P("leaf", None, "front"),
    )
    return jax.shard_map(
        on_device, mesh=mesh, in_specs=placed, out_specs=P("leaf", None, "front"), check_vma=False
    )
```

time: 348 us -> 97 us (0.28)
  the two profiles are of different devices: /device:TPU:4 before, /device:TPU:0 now
where the time goes in v1:
time: 97 us; the launch traced here: 96.7 us
  Pallas kernels  89.9 us (93%)
  local copies, waits for them, and re-layouts  6.72 us (7%)
    pallas_call x1, Pallas kernels, on_device(): pl.pallas_call(functools.partial(kernel, leaves, fronts), out_shape=jax.S...  89.9 us
    unnamed x13, local copies, waits for them, and re-layouts  6.72 us

profile of v1, /device:TPU:0, one launch (start us, length us, event | category | flops | bytes accessed | tf_op | source)
XLA Modules:
  0.0 96.7 jit_solution(15170145656062349122)
XLA Ops:
  0.0 0.0 copy-start
  0.0 1.4 %copy-done = bf16[1,3,512,512]{3,2,1,0:T(8,128)(2,1)S(1)} copy-done((bf16[1,3,512,512]{3,2,1,0:T(8,128)(2,1)S(1)}, bf16[1,3,512,512]{3,2,1,0:T(8,128)(2,1)}, u32[]{:S(2)}) %copy-start) | copy-done | bytes 1572888
  1.4 0.0 copy-start.1
  1.4 1.0 %copy-done.1 = bf16[1,1536,128]{2,1,0:T(8,128)(2,1)S(1)} copy-done((bf16[1,1536,128]{2,1,0:T(8,128)(2,1)S(1)}, bf16[1,1536,128]{2,1,0:T(8,128)(2,1)}, u32[]{:S(2)}) %copy-start.1) | copy-done | bytes 393240
  2.4 0.0 copy-start.2
  2.4 1.0 %copy-done.2 = bf16[1,1536,128]{2,1,0:T(8,128)(2,1)S(1)} copy-done((bf16[1,1536,128]{2,1,0:T(8,128)(2,1)S(1)}, bf16[1,1536,128]{2,1,0:T(8,128)(2,1)}, u32[]{:S(2)}) %copy-start.2) | copy-done | bytes 393240
  3.4 0.0 copy-start.3
  3.4 1.0 %copy-done.3 = bf16[1536,128]{1,0:T(8,128)(2,1)S(1)} copy-done((bf16[1536,128]{1,0:T(8,128)(2,1)S(1)}, bf16[1536,128]{1,0:T(8,128)(2,1)}, u32[]{:S(2)}) %copy-start.3) | copy-done | bytes 393240
  4.4 0.0 copy-start.4
  4.4 0.9 copy-done.4
  5.3 0.0 copy-start.5
  5.3 0.7 copy-done.5
  6.0 89.9 %shard_map.64 = f32[1,64,1536]{2,1,0:T(8,128)S(1)} custom-call(s32[1,3]{1,0:T(1,128)S(1)} %copy-done.5, bf16[1,1536,128]{2,1,0:T(8,128)(2,1)S(1)} %copy-done.1, bf16[1,1536,128]{2,1,0:T(8,128)(2,1)S(1)} %copy-done.2, bf16[1536,128]{1,0:T(8,128)(2,1)S(1)} %copy-done.3, bf16[1,3,512,512]{3,2,1,0:T(8,128)(2,1)S(1)} %copy-done, bf16[1,64,1536]{2,1,0:T(8,128)(2,1)S(1)} %copy-done.4), custom_call_target="tpu_custom_call" | custom-call | tf_op jit(solution)/shard_map/pallas_call | solution.py:360
  95.9 0.7 copy.8
Async XLA Ops:
  0.0 1.4 %copy-start = (bf16[1,3,512,512]{3,2,1,0:T(8,128)(2,1)S(1)}, bf16[1,3,512,512]{3,2,1,0:T(8,128)(2,1)}, u32[]{:S(2)}) copy-start(bf16[1,3,512,512]{3,2,1,0:T(8,128)(2,1)} %dinv_ref.1) | copy-start | bytes 4718596
  1.4 1.0 %copy-start.1 = (bf16[1,1536,128]{2,1,0:T(8,128)(2,1)S(1)}, bf16[1,1536,128]{2,1,0:T(8,128)(2,1)}, u32[]{:S(2)}) copy-start(bf16[1,1536,128]{2,1,0:T(8,128)(2,1)} %u_ref.1) | copy-start | bytes 1179652
  2.4 1.0 %copy-start.2 = (bf16[1,1536,128]{2,1,0:T(8,128)(2,1)S(1)}, bf16[1,1536,128]{2,1,0:T(8,128)(2,1)}, u32[]{:S(2)}) copy-start(bf16[1,1536,128]{2,1,0:T(8,128)(2,1)} %v_ref.1) | copy-start | bytes 1179652
  3.4 1.0 %copy-start.3 = (bf16[1536,128]{1,0:T(8,128)(2,1)S(1)}, bf16[1536,128]{1,0:T(8,128)(2,1)}, u32[]{:S(2)}) copy-start(bf16[1536,128]{1,0:T(8,128)(2,1)} %sketch_ref.1) | copy-start | bytes 1179652
  4.4 0.9 copy-start.4
  5.3 0.7 copy-start.5

commit v2 on v1

--- a/solution.py
+++ b/solution.py
@@ -10,7 +10,7 @@
 MESH = pl.DeviceIdType.MESH
 F32 = jnp.float32
 BF16 = jnp.bfloat16
-PANEL = 8
+PANEL = 16
 
 
 def dot(a, b):
@@ -25,12 +25,25 @@
     return lax.dot_general(a, b, (((0,), (0,)), ((), ())), preferred_element_type=F32)
 
 
+def thirds(x):
+    high = x.astype(BF16)
+    rest = x - high.astype(F32)
+    middle = rest.astype(BF16)
+    return high, middle, (rest - middle.astype(F32)).astype(BF16)
+
+
 def full(a, b, ca=1, cb=0):
+    if a.dtype == BF16:
+        pa, pb = [a] * 3, thirds(b)
+    elif b.dtype == BF16:
+        pa, pb = thirds(a), [b] * 3
+    else:
+        (a1, a2, a3), (b1, b2, b3) = thirds(a), thirds(b)
+        pa, pb = (a1, a2, a1, a3, a2, a1), (b1, b1, b2, b1, b2, b3)
     return lax.dot_general(
-        a,
-        b,
+        jnp.concatenate(pa, axis=ca),
+        jnp.concatenate(pb, axis=cb),
         (((ca,), (cb,)), ((), ())),
-        precision=lax.Precision.HIGHEST,
         preferred_element_type=F32,
     )
 
@@ -85,7 +98,7 @@
             work[q] -= full(below, jnp.concatenate([left, right], axis=1), 0, 0)
         return carry
 
-    lax.fori_loop(0, size // PANEL, step, 0)
+    lax.fori_loop(0, size // PANEL, step, 0, unroll=True)
 
 
 def kernel(
@@ -238,21 +251,21 @@
         between = block(a, 2)
         pair = square(block(a, 1), between, between.T, block(b, 1))
         raw.append(jnp.concatenate([block(a, 0), block(b, 0)], axis=0))
-        small.append(raw[p].astype(BF16).astype(F32))
+        small.append(raw[p].astype(BF16))
         cross.append(full(pair, small[p]))
         grams.append(full(small[p], cross[p], 0, 0))
     inverse_factors(grams, work, inverse)
     turn = [full(small[p], inverse[p], 1, 1) for p in range(2)]
-    weight = [full(cross[p], inverse[p], 1, 1).astype(BF16).astype(F32) for p in range(2)]
-    small2 = [full(weight[p], raw[p], 0, 0).astype(BF16).astype(F32) for p in range(2)]
+    weight = [full(cross[p], inverse[p], 1, 1).astype(BF16) for p in range(2)]
+    small2 = [full(weight[p], raw[p], 0, 0).astype(BF16) for p in range(2)]
     pair = square(block(0, 3), block(3, 2).T, block(1, 2), block(1, 3))
     middle = full(turn[0], full(pair, turn[1]), 0, 0)
-    cross2 = [small2[0] + full(middle, small2[1]), full(middle, small2[0], 0, 0) + small2[1]]
+    cross2 = [small2[0].astype(F32) + full(middle, small2[1]), full(middle, small2[0], 0, 0) + small2[1].astype(F32)]
     gram2 = full(small2[0], cross2[0], 0, 0) + full(small2[1], cross2[1], 0, 0)
     inverse_factors([gram2], work, inverse)
     turn2 = [halves(full(turn[p], full(small2[p], inverse[0], 1, 1))) for p in range(2)]
     weight2 = [
-        halves(full(weight[p], full(cross2[p], inverse[0], 1, 1).astype(BF16).astype(F32))) for p in range(2)
+        halves(dot(weight[p], full(cross2[p], inverse[0], 1, 1).astype(BF16))) for p in range(2)
     ]
 
     def combined(held, factors):

time: 97 us -> 76.9 us (0.79)
  Pallas kernels: 89.9 us -> 69.8 us
    pallas_call x1, Pallas kernels: 89.9 us -> 69.8 us  [on_device(): pl.pallas_call(functools.partial(kernel, leaves, fronts), out_shape=jax.S...]
where the time goes in v2:
time: 76.9 us; the launch traced here: 76.6 us
  Pallas kernels  69.8 us (91%)
  local copies, waits for them, and re-layouts  6.72 us (9%)
    pallas_call x1, Pallas kernels, on_device(): pl.pallas_call(functools.partial(kernel, leaves, fronts), out_shape=jax.S...  69.8 us
    unnamed x13, local copies, waits for them, and re-layouts  6.72 us

profile of v2, /device:TPU:0, one launch (start us, length us, event | category | flops | bytes accessed | tf_op | source)
XLA Modules:
  0.0 76.6 jit_solution(3178796711061194775)
XLA Ops:
  0.0 0.0 copy-start
  0.0 1.4 %copy-done = bf16[1,3,512,512]{3,2,1,0:T(8,128)(2,1)S(1)} copy-done((bf16[1,3,512,512]{3,2,1,0:T(8,128)(2,1)S(1)}, bf16[1,3,512,512]{3,2,1,0:T(8,128)(2,1)}, u32[]{:S(2)}) %copy-start) | copy-done | bytes 1572888
  1.4 0.0 copy-start.1
  1.4 1.0 %copy-done.1 = bf16[1,1536,128]{2,1,0:T(8,128)(2,1)S(1)} copy-done((bf16[1,1536,128]{2,1,0:T(8,128)(2,1)S(1)}, bf16[1,1536,128]{2,1,0:T(8,128)(2,1)}, u32[]{:S(2)}) %copy-start.1) | copy-done | bytes 393240
  2.4 0.0 copy-start.2
  2.4 1.0 %copy-done.2 = bf16[1,1536,128]{2,1,0:T(8,128)(2,1)S(1)} copy-done((bf16[1,1536,128]{2,1,0:T(8,128)(2,1)S(1)}, bf16[1,1536,128]{2,1,0:T(8,128)(2,1)}, u32[]{:S(2)}) %copy-start.2) | copy-done | bytes 393240
  3.4 0.0 copy-start.3
  3.4 1.0 %copy-done.3 = bf16[1536,128]{1,0:T(8,128)(2,1)S(1)} copy-done((bf16[1536,128]{1,0:T(8,128)(2,1)S(1)}, bf16[1536,128]{1,0:T(8,128)(2,1)}, u32[]{:S(2)}) %copy-start.3) | copy-done | bytes 393240
  4.4 0.0 copy-start.4
  4.4 0.9 %copy-done.4 = bf16[1,64,1536]{2,1,0:T(8,128)(2,1)S(1)} copy-done((bf16[1,64,1536]{2,1,0:T(8,128)(2,1)S(1)}, bf16[1,64,1536]{2,1,0:T(8,128)(2,1)}, u32[]{:S(2)}) %copy-start.4) | copy-done | bytes 196632
  5.3 0.0 copy-start.5
  5.3 0.7 copy-done.5
  6.0 69.8 %shard_map.64 = f32[1,64,1536]{2,1,0:T(8,128)S(1)} custom-call(s32[1,3]{1,0:T(1,128)S(1)} %copy-done.5, bf16[1,1536,128]{2,1,0:T(8,128)(2,1)S(1)} %copy-done.1, bf16[1,1536,128]{2,1,0:T(8,128)(2,1)S(1)} %copy-done.2, bf16[1536,128]{1,0:T(8,128)(2,1)S(1)} %copy-done.3, bf16[1,3,512,512]{3,2,1,0:T(8,128)(2,1)S(1)} %copy-done, bf16[1,64,1536]{2,1,0:T(8,128)(2,1)S(1)} %copy-done.4), custom_call_target="tpu_custom_call" | custom-call | tf_op jit(solution)/shard_map/pallas_call | solution.py:373
  75.8 0.7 copy.8
Async XLA Ops:
  0.0 1.4 %copy-start = (bf16[1,3,512,512]{3,2,1,0:T(8,128)(2,1)S(1)}, bf16[1,3,512,512]{3,2,1,0:T(8,128)(2,1)}, u32[]{:S(2)}) copy-start(bf16[1,3,512,512]{3,2,1,0:T(8,128)(2,1)} %dinv_ref.1) | copy-start | bytes 4718596
  1.4 1.0 %copy-start.1 = (bf16[1,1536,128]{2,1,0:T(8,128)(2,1)S(1)}, bf16[1,1536,128]{2,1,0:T(8,128)(2,1)}, u32[]{:S(2)}) copy-start(bf16[1,1536,128]{2,1,0:T(8,128)(2,1)} %u_ref.1) | copy-start | bytes 1179652
  2.4 1.0 %copy-start.2 = (bf16[1,1536,128]{2,1,0:T(8,128)(2,1)S(1)}, bf16[1,1536,128]{2,1,0:T(8,128)(2,1)}, u32[]{:S(2)}) copy-start(bf16[1,1536,128]{2,1,0:T(8,128)(2,1)} %v_ref.1) | copy-start | bytes 1179652
  3.4 1.0 %copy-start.3 = (bf16[1536,128]{1,0:T(8,128)(2,1)S(1)}, bf16[1536,128]{1,0:T(8,128)(2,1)}, u32[]{:S(2)}) copy-start(bf16[1536,128]{1,0:T(8,128)(2,1)} %sketch_ref.1) | copy-start | bytes 1179652
  4.4 0.9 %copy-start.4 = (bf16[1,64,1536]{2,1,0:T(8,128)(2,1)S(1)}, bf16[1,64,1536]{2,1,0:T(8,128)(2,1)}, u32[]{:S(2)}) copy-start(bf16[1,64,1536]{2,1,0:T(8,128)(2,1)} %rhs_ref.1) | copy-start | bytes 589828
  5.3 0.7 copy-start.5

commit v3 on v2

--- a/solution.py
+++ b/solution.py
@@ -33,7 +33,9 @@
 
 
 def full(a, b, ca=1, cb=0):
-    if a.dtype == BF16:
+    if a.dtype == BF16 and b.dtype == BF16:
+        pa, pb = [a], [b]
+    elif a.dtype == BF16:
         pa, pb = [a] * 3, thirds(b)
     elif b.dtype == BF16:
         pa, pb = thirds(a), [b] * 3
@@ -299,7 +301,7 @@
             piece2(front), piece2(front), ag2_send.at[d], ag2_recv.at[d], (leaf, lax.rem(front + d, fronts))
         )
 
-    whole[pl.ds(pl.multiple_of(front * shard2, 8), shard2), :] = reduced(*second)
+    whole[pl.ds(pl.multiple_of(front * shard2, 16), shard2), :] = reduced(*second).astype(BF16)
     for d in range(1, fronts):
         gather2_copy(d).start()
     for d in range(1, fronts):
@@ -311,7 +313,7 @@
     prefix = jnp.where(low == along, 1.0, 0.0)
 
     def then(first_map, second_map):
-        return full(first_map, second_map[:rank]) + jnp.where(low >= rank, second_map, 0.0)
+        return full(first_map.astype(BF16), second_map[:rank]) + jnp.where(low >= rank, second_map.astype(F32), 0.0)
 
     def hyper_copy(k):
         send = pl.ds(0, used) if k < levels - 1 else pl.ds(rank, sides)
@@ -325,8 +327,8 @@
         hyper_copy(k).wait_recv()
         upper = lax.rem(leaf // (1 << k), 2) == 1
         if k < levels - 1:
-            here, there = hyper[k, 0], hyper[k, 1]
-            hyper[k + 1, 0] = then(jnp.where(upper, there, here), jnp.where(upper, here, there))
+            here, there = hyper[k, 0].astype(F32), hyper[k, 1].astype(F32)
+            hyper[k + 1, 0] = then(jnp.where(upper, there, here), jnp.where(upper, here, there).astype(BF16)).astype(BF16)
             prefix = jnp.where(upper, then(there, prefix), prefix)
         else:
             there = hyper[k, 1, pl.ds(rank, sides), :]
@@ -367,7 +369,7 @@
         sides = rhs.shape[1]
         used = rank + sides
         shard = 4 * rank // fronts
-        shard2 = -(-used // (8 * fronts)) * 8
+        shard2 = -(-used // (16 * fronts)) * 16
         vmem = pl.BlockSpec(memory_space=pltpu.VMEM)
         dma = pltpu.SemaphoreType.DMA
         return pl.pallas_call(
@@ -386,8 +388,8 @@
                 pltpu.VMEM((2 * rank, 2 * rank), F32),
                 pltpu.VMEM((shard2 * fronts, rank), F32),
                 pltpu.VMEM((fronts, shard2, rank), F32),
-                pltpu.VMEM((shard2 * fronts, rank), F32),
-                pltpu.VMEM((levels, 2, used, rank), F32),
+                pltpu.VMEM((shard2 * fronts, rank), BF16),
+                pltpu.VMEM((levels, 2, used, rank), BF16),
                 pltpu.VMEM((sides, length), F32),
                 dma((2, 3, tiles)),
                 dma((2, 3, tiles)),

time: 76.9 us -> 75.4 us (0.980)
  Pallas kernels: 69.8 us -> 68.3 us
    pallas_call x1, Pallas kernels: 69.8 us -> 68.3 us  [on_device(): pl.pallas_call(functools.partial(kernel, leaves, fronts), out_shape=jax.S...]
where the time goes in v3:
time: 75.4 us; the launch traced here: 75.1 us
  Pallas kernels  68.3 us (91%)
  local copies, waits for them, and re-layouts  6.72 us (9%)
    pallas_call x1, Pallas kernels, on_device(): pl.pallas_call(functools.partial(kernel, leaves, fronts), out_shape=jax.S...  68.3 us
    unnamed x13, local copies, waits for them, and re-layouts  6.72 us

profile of v3, /device:TPU:0, one launch (start us, length us, event | category | flops | bytes accessed | tf_op | source)
XLA Modules:
  0.0 75.1 jit_solution(3595075621658962522)
XLA Ops:
  0.0 0.0 copy-start
  0.0 1.4 %copy-done = bf16[1,3,512,512]{3,2,1,0:T(8,128)(2,1)S(1)} copy-done((bf16[1,3,512,512]{3,2,1,0:T(8,128)(2,1)S(1)}, bf16[1,3,512,512]{3,2,1,0:T(8,128)(2,1)}, u32[]{:S(2)}) %copy-start) | copy-done | bytes 1572888
  1.4 0.0 copy-start.1
  1.4 1.0 %copy-done.1 = bf16[1,1536,128]{2,1,0:T(8,128)(2,1)S(1)} copy-done((bf16[1,1536,128]{2,1,0:T(8,128)(2,1)S(1)}, bf16[1,1536,128]{2,1,0:T(8,128)(2,1)}, u32[]{:S(2)}) %copy-start.1) | copy-done | bytes 393240
  2.4 0.0 copy-start.2
  2.4 1.0 %copy-done.2 = bf16[1,1536,128]{2,1,0:T(8,128)(2,1)S(1)} copy-done((bf16[1,1536,128]{2,1,0:T(8,128)(2,1)S(1)}, bf16[1,1536,128]{2,1,0:T(8,128)(2,1)}, u32[]{:S(2)}) %copy-start.2) | copy-done | bytes 393240
  3.4 0.0 copy-start.3
  3.4 1.0 %copy-done.3 = bf16[1536,128]{1,0:T(8,128)(2,1)S(1)} copy-done((bf16[1536,128]{1,0:T(8,128)(2,1)S(1)}, bf16[1536,128]{1,0:T(8,128)(2,1)}, u32[]{:S(2)}) %copy-start.3) | copy-done | bytes 393240
  4.4 0.0 copy-start.4
  4.4 0.9 %copy-done.4 = bf16[1,64,1536]{2,1,0:T(8,128)(2,1)S(1)} copy-done((bf16[1,64,1536]{2,1,0:T(8,128)(2,1)S(1)}, bf16[1,64,1536]{2,1,0:T(8,128)(2,1)}, u32[]{:S(2)}) %copy-start.4) | copy-done | bytes 196632
  5.3 0.0 copy-start.5
  5.3 0.7 copy-done.5
  6.0 68.3 %shard_map.64 = f32[1,64,1536]{2,1,0:T(8,128)S(1)} custom-call(s32[1,3]{1,0:T(1,128)S(1)} %copy-done.5, bf16[1,1536,128]{2,1,0:T(8,128)(2,1)S(1)} %copy-done.1, bf16[1,1536,128]{2,1,0:T(8,128)(2,1)S(1)} %copy-done.2, bf16[1536,128]{1,0:T(8,128)(2,1)S(1)} %copy-done.3, bf16[1,3,512,512]{3,2,1,0:T(8,128)(2,1)S(1)} %copy-done, bf16[1,64,1536]{2,1,0:T(8,128)(2,1)S(1)} %copy-done.4), custom_call_target="tpu_custom_call" | custom-call | tf_op jit(solution)/shard_map/pallas_call | solution.py:375
  74.3 0.7 copy.8
Async XLA Ops:
  0.0 1.4 %copy-start = (bf16[1,3,512,512]{3,2,1,0:T(8,128)(2,1)S(1)}, bf16[1,3,512,512]{3,2,1,0:T(8,128)(2,1)}, u32[]{:S(2)}) copy-start(bf16[1,3,512,512]{3,2,1,0:T(8,128)(2,1)} %dinv_ref.1) | copy-start | bytes 4718596
  1.4 1.0 %copy-start.1 = (bf16[1,1536,128]{2,1,0:T(8,128)(2,1)S(1)}, bf16[1,1536,128]{2,1,0:T(8,128)(2,1)}, u32[]{:S(2)}) copy-start(bf16[1,1536,128]{2,1,0:T(8,128)(2,1)} %u_ref.1) | copy-start | bytes 1179652
  2.4 1.0 %copy-start.2 = (bf16[1,1536,128]{2,1,0:T(8,128)(2,1)S(1)}, bf16[1,1536,128]{2,1,0:T(8,128)(2,1)}, u32[]{:S(2)}) copy-start(bf16[1,1536,128]{2,1,0:T(8,128)(2,1)} %v_ref.1) | copy-start | bytes 1179652
  3.4 1.0 %copy-start.3 = (bf16[1536,128]{1,0:T(8,128)(2,1)S(1)}, bf16[1536,128]{1,0:T(8,128)(2,1)}, u32[]{:S(2)}) copy-start(bf16[1536,128]{1,0:T(8,128)(2,1)} %sketch_ref.1) | copy-start | bytes 1179652
  4.4 0.9 %copy-start.4 = (bf16[1,64,1536]{2,1,0:T(8,128)(2,1)S(1)}, bf16[1,64,1536]{2,1,0:T(8,128)(2,1)}, u32[]{:S(2)}) copy-start(bf16[1,64,1536]{2,1,0:T(8,128)(2,1)} %rhs_ref.1) | copy-start | bytes 589828
  5.3 0.7 copy-start.5

commit v4 on v3

--- a/solution.py
+++ b/solution.py
@@ -190,20 +190,20 @@
         scatter((j + 1) * fronts // 4, (j + 2) * fronts // 4, first)
 
     def reduced(buffer, landing, size, send, recv):
-        total = buffer[pl.ds(pl.multiple_of(front * size, 8), size), :]
+        total = buffer[pl.ds(pl.multiple_of(front * size, 16), size), :].astype(F32)
         for s in range(fronts):
             @pl.when(front != s)
             def _(s=s):
                 landing_wait(s, buffer, landing, size, send, recv)
 
-            total = total + jnp.where(front != s, landing[s], 0.0)
+            total = total + jnp.where(front != s, landing[s].astype(F32), 0.0)
         return total
 
     for s in range(fronts):
         @pl.when(front == s)
         def _(s=s):
             landed[s] = jnp.zeros(landed.shape[1:], F32)
-            landed2[s] = jnp.zeros(landed2.shape[1:], F32)
+            landed2[s] = jnp.zeros(landed2.shape[1:], BF16)
 
     def piece(i, s):
         return gath.at[i, pl.ds(s * shard, shard), :]
@@ -287,9 +287,9 @@
     right_f = combined(vall, weight2)
     used = rank + sides
     if used < part.shape[0]:
-        part[pl.ds(used, part.shape[0] - used), :] = jnp.zeros((part.shape[0] - used, rank), F32)
-    part[pl.ds(0, rank), :] = -dot_tn(jnp.concatenate(coupled, axis=0), right_f)
-    part[pl.ds(rank, sides), :] = dot(sol[...].astype(BF16), right_f)
+        part[pl.ds(used, part.shape[0] - used), :] = jnp.zeros((part.shape[0] - used, rank), BF16)
+    part[pl.ds(0, rank), :] = (-dot_tn(jnp.concatenate(coupled, axis=0), right_f)).astype(BF16)
+    part[pl.ds(rank, sides), :] = dot(sol[...].astype(BF16), right_f).astype(BF16)
 
     scatter(0, fronts, second)
 
@@ -386,8 +386,8 @@
                 pltpu.VMEM((2, rank, 2 * rank), F32),
                 pltpu.VMEM((2, rank, rank), F32),
                 pltpu.VMEM((2 * rank, 2 * rank), F32),
-                pltpu.VMEM((shard2 * fronts, rank), F32),
-                pltpu.VMEM((fronts, shard2, rank), F32),
+                pltpu.VMEM((shard2 * fronts, rank), BF16),
+                pltpu.VMEM((fronts, shard2, rank), BF16),
                 pltpu.VMEM((shard2 * fronts, rank), BF16),
                 pltpu.VMEM((levels, 2, used, rank), BF16),
                 pltpu.VMEM((sides, length), F32),

time: 75.4 us -> 75 us (level)
  no operation moved by 1% of the time
where the time goes in v4:
time: 75 us; the launch traced here: 74.7 us
  Pallas kernels  68 us (91%)
  local copies, waits for them, and re-layouts  6.72 us (9%)
    pallas_call x1, Pallas kernels, on_device(): pl.pallas_call(functools.partial(kernel, leaves, fronts), out_shape=jax.S...  68 us
    unnamed x13, local copies, waits for them, and re-layouts  6.72 us

profile of v4, /device:TPU:0, one launch (start us, length us, event | category | flops | bytes accessed | tf_op | source)
XLA Modules:
  0.0 74.7 jit_solution(14012701178751815844)
XLA Ops:
  0.0 0.0 copy-start
  0.0 1.4 %copy-done = bf16[1,3,512,512]{3,2,1,0:T(8,128)(2,1)S(1)} copy-done((bf16[1,3,512,512]{3,2,1,0:T(8,128)(2,1)S(1)}, bf16[1,3,512,512]{3,2,1,0:T(8,128)(2,1)}, u32[]{:S(2)}) %copy-start) | copy-done | bytes 1572888
  1.4 0.0 copy-start.1
  1.4 1.0 %copy-done.1 = bf16[1,1536,128]{2,1,0:T(8,128)(2,1)S(1)} copy-done((bf16[1,1536,128]{2,1,0:T(8,128)(2,1)S(1)}, bf16[1,1536,128]{2,1,0:T(8,128)(2,1)}, u32[]{:S(2)}) %copy-start.1) | copy-done | bytes 393240
  2.4 0.0 copy-start.2
  2.4 1.0 %copy-done.2 = bf16[1,1536,128]{2,1,0:T(8,128)(2,1)S(1)} copy-done((bf16[1,1536,128]{2,1,0:T(8,128)(2,1)S(1)}, bf16[1,1536,128]{2,1,0:T(8,128)(2,1)}, u32[]{:S(2)}) %copy-start.2) | copy-done | bytes 393240
  3.4 0.0 copy-start.3
  3.4 1.0 %copy-done.3 = bf16[1536,128]{1,0:T(8,128)(2,1)S(1)} copy-done((bf16[1536,128]{1,0:T(8,128)(2,1)S(1)}, bf16[1536,128]{1,0:T(8,128)(2,1)}, u32[]{:S(2)}) %copy-start.3) | copy-done | bytes 393240
  4.4 0.0 copy-start.4
  4.4 0.9 %copy-done.4 = bf16[1,64,1536]{2,1,0:T(8,128)(2,1)S(1)} copy-done((bf16[1,64,1536]{2,1,0:T(8,128)(2,1)S(1)}, bf16[1,64,1536]{2,1,0:T(8,128)(2,1)}, u32[]{:S(2)}) %copy-start.4) | copy-done | bytes 196632
  5.3 0.0 copy-start.5
  5.3 0.7 copy-done.5
  6.0 68.0 %shard_map.64 = f32[1,64,1536]{2,1,0:T(8,128)S(1)} custom-call(s32[1,3]{1,0:T(1,128)S(1)} %copy-done.5, bf16[1,1536,128]{2,1,0:T(8,128)(2,1)S(1)} %copy-done.1, bf16[1,1536,128]{2,1,0:T(8,128)(2,1)S(1)} %copy-done.2, bf16[1536,128]{1,0:T(8,128)(2,1)S(1)} %copy-done.3, bf16[1,3,512,512]{3,2,1,0:T(8,128)(2,1)S(1)} %copy-done, bf16[1,64,1536]{2,1,0:T(8,128)(2,1)S(1)} %copy-done.4), custom_call_target="tpu_custom_call" | custom-call | tf_op jit(solution)/shard_map/pallas_call | solution.py:375
  73.9 0.7 %copy.8 = f32[1,64,1536]{2,1,0:T(8,128)} copy(f32[1,64,1536]{2,1,0:T(8,128)S(1)} %shard_map.64) | data formatting | bytes 786432
Async XLA Ops:
  0.0 1.4 %copy-start = (bf16[1,3,512,512]{3,2,1,0:T(8,128)(2,1)S(1)}, bf16[1,3,512,512]{3,2,1,0:T(8,128)(2,1)}, u32[]{:S(2)}) copy-start(bf16[1,3,512,512]{3,2,1,0:T(8,128)(2,1)} %dinv_ref.1) | copy-start | bytes 4718596
  1.4 1.0 %copy-start.1 = (bf16[1,1536,128]{2,1,0:T(8,128)(2,1)S(1)}, bf16[1,1536,128]{2,1,0:T(8,128)(2,1)}, u32[]{:S(2)}) copy-start(bf16[1,1536,128]{2,1,0:T(8,128)(2,1)} %u_ref.1) | copy-start | bytes 1179652
  2.4 1.0 %copy-start.2 = (bf16[1,1536,128]{2,1,0:T(8,128)(2,1)S(1)}, bf16[1,1536,128]{2,1,0:T(8,128)(2,1)}, u32[]{:S(2)}) copy-start(bf16[1,1536,128]{2,1,0:T(8,128)(2,1)} %v_ref.1) | copy-start | bytes 1179652
  3.4 1.0 %copy-start.3 = (bf16[1536,128]{1,0:T(8,128)(2,1)S(1)}, bf16[1536,128]{1,0:T(8,128)(2,1)}, u32[]{:S(2)}) copy-start(bf16[1536,128]{1,0:T(8,128)(2,1)} %sketch_ref.1) | copy-start | bytes 1179652
  4.4 0.9 %copy-start.4 = (bf16[1,64,1536]{2,1,0:T(8,128)(2,1)S(1)}, bf16[1,64,1536]{2,1,0:T(8,128)(2,1)}, u32[]{:S(2)}) copy-start(bf16[1,64,1536]{2,1,0:T(8,128)(2,1)} %rhs_ref.1) | copy-start | bytes 589828
  5.3 0.7 copy-start.5
